TPU v7x, 32 devices: a whole 2x2x4 slice. The times are simulated.
32 devices in a mesh: section: 2 (over core), dp: 16 (over z, y, x).
Axes of the slice: x: 2, y: 2, z: 4, core: 2. Of those that a mesh axis runs over, the one named last changes fastest.
Arguments:
- media: bfloat16 [128, 256, 1024], P('dp'), may hold values from -6 to 6
- image_live: int32 [128], P('dp'), may hold values 0 or 1
- start_latents: bfloat16 [64, 1024], replicated, may hold values from -6 to 6
- latent_cotangent: bfloat16 [128, 64, 1024], P('dp'), may hold values from -6 to 6
- media_gain: float32 [2, 1024], P('section'), may hold values from 0.5 to 1.5
- media_bias: float32 [2, 1024], P('section'), may hold values from -1.5 to 1.5
- latent_gain: float32 [2, 1024], P('section'), may hold values from 0.5 to 1.5
- latent_bias: float32 [2, 1024], P('section'), may hold values from -1.5 to 1.5
- w_query: bfloat16 [2, 1024, 512], P('section'), may hold values from -0.1875 to 0.1875
- w_kv: bfloat16 [2, 1024, 1024], P('section'), may hold values from -0.1875 to 0.1875
- w_out: bfloat16 [2, 512, 1024], P('section'), may hold values from -3 to 3
- ff_gain: float32 [2, 1024], P('section'), may hold values from 0.5 to 1.5
- ff_bias: float32 [2, 1024], P('section'), may hold values from -1.5 to 1.5
- w_up: bfloat16 [2, 1024, 4096], P('section'), may hold values from -0.1875 to 0.1875
- w_down: bfloat16 [2, 4096, 1024], P('section'), may hold values from -0.09375 to 0.09375
Outputs:
- layer_latents: bfloat16 [2, 128, 64, 1024], P('section', 'dp')
- media_grad: float32 [128, 256, 1024], P('dp', None, 'section')
- start_grad: float32 [64, 1024], P('section', 'dp')
- grad_media_gain: float32 [2, 1024], P('section', 'dp')
- grad_media_bias: float32 [2, 1024], P('section', 'dp')
- grad_latent_gain: float32 [2, 1024], P('section', 'dp')
- grad_latent_bias: float32 [2, 1024], P('section', 'dp')
- grad_query: float32 [2, 1024, 512], P('section', 'dp')
- grad_kv: float32 [2, 1024, 1024], P('section', 'dp')
- grad_out: float32 [2, 512, 1024], P('section', 'dp')
- grad_ff_gain: float32 [2, 1024], P('section', 'dp')
- grad_ff_bias: float32 [2, 1024], P('section', 'dp')
- grad_up: float32 [2, 1024, 4096], P('section', 'dp')
- grad_down: float32 [2, 4096, 1024], P('section', 'dp')
All inputs are finite; a program needn't handle non-finite values. No bound on the sum of `image_live` on one device may be relied on, other than what follows from the above.
Results may differ from a plain program's by a relative error of at most 0.017.
Values may be sent and summed in bfloat16 or wider, within the bound.
A program may use at most 320 MiB of HBM per device.

v0:
```python
import jax
import jax.numpy as jnp
from jax import lax
from jax.sharding import PartitionSpec as P

HEADS = 8
HEAD_DIM = 64
MB = 4


def shifted(x, axis, by):
    peers = lax.axis_size(axis)
    pairs = [(i, i + by) for i in range(peers) if 0 <= i + by < peers]
    return lax.ppermute(x, axis, pairs)


def product(form, left, right):
    return jnp.einsum(form, left, right, preferred_element_type=jnp.float32)


def layer_norm(value, gain, offset):
    centred = value - jnp.mean(value, axis=-1, keepdims=True)
    factor = lax.rsqrt(jnp.mean(centred * centred, axis=-1, keepdims=True) + 1e-05)
    normed = centred * factor
    return (normed * gain + offset, normed, factor)


def norm_back(upstream, normed, factor, gain):
    scaled = upstream * gain
    inner = factor * (
        scaled
        - jnp.mean(scaled, axis=-1, keepdims=True)
        - normed * jnp.mean(scaled * normed, axis=-1, keepdims=True)
    )
    return (inner, jnp.sum(upstream * normed, axis=(0, 1)), jnp.sum(upstream, axis=(0, 1)))


def split_heads(values):
    return values.reshape(values.shape[0], values.shape[1], HEADS, -1)


def layer_forward(latent, media_rows, params):
    (
        media_gain,
        media_bias,
        latent_gain,
        latent_bias,
        w_query,
        w_kv,
        w_out,
        ff_gain,
        ff_bias,
        w_up,
        w_down,
    ) = params
    inner_width = w_query.shape[1]
    norm_media, media_hat, media_factor = layer_norm(
        media_rows.astype(jnp.float32), media_gain, media_bias
    )
    norm_latent, latent_hat, latent_factor = layer_norm(latent, latent_gain, latent_bias)
    latent_low = norm_latent.astype(jnp.bfloat16)
    query = (product("bld,de->ble", latent_low, w_query) * HEAD_DIM ** (-0.5)).astype(jnp.bfloat16)
    joined = jnp.concatenate([norm_media.astype(jnp.bfloat16), latent_low], axis=1)
    keyval = product("bnd,de->bne", joined, w_kv).astype(jnp.bfloat16)
    scores = product("blhe,bnhe->bhln", split_heads(query), split_heads(keyval[..., :inner_width]))
    row_max = jnp.max(scores, axis=-1, keepdims=True)
    exponent = jnp.exp(scores - row_max)
    row_total = jnp.sum(exponent, axis=-1, keepdims=True)
    attn_prob = exponent / row_total
    log_total = row_max + jnp.log(row_total)
    attended = product(
        "bhln,bnhe->blhe", attn_prob.astype(jnp.bfloat16), split_heads(keyval[..., inner_width:])
    )
    attended = attended.reshape(latent.shape[0], latent.shape[1], inner_width).astype(jnp.bfloat16)
    mixed = latent + product("ble,ed->bld", attended, w_out)
    norm_ff, ff_hat, ff_factor = layer_norm(mixed, ff_gain, ff_bias)
    ff_input = norm_ff.astype(jnp.bfloat16)
    pre_act = product("bld,df->blf", ff_input, w_up)
    hidden = jax.nn.gelu(pre_act, approximate=False).astype(jnp.bfloat16)
    result = mixed + product("blf,fd->bld", hidden, w_down)
    kept = (
        media_hat,
        media_factor,
        latent_hat,
        latent_factor,
        query,
        joined,
        keyval,
        log_total,
        attended,
        ff_hat,
        ff_factor,
        ff_input,
        pre_act,
        hidden,
    )
    return (result, kept)


def layer_backward(kept, upstream, params):
    (
        media_gain,
        media_bias,
        latent_gain,
        latent_bias,
        w_query,
        w_kv,
        w_out,
        ff_gain,
        ff_bias,
        w_up,
        w_down,
    ) = params
    (
        media_hat,
        media_factor,
        latent_hat,
        latent_factor,
        query,
        joined,
        keyval,
        log_total,
        attended,
        ff_hat,
        ff_factor,
        ff_input,
        pre_act,
        hidden,
    ) = kept
    inner_width = w_query.shape[1]
    patch_rows = joined.shape[1] - upstream.shape[1]
    upstream_low = upstream.astype(jnp.bfloat16)
    grad_down = product("blf,bld->fd", hidden, upstream_low)
    grad_hidden = product("bld,fd->blf", upstream_low, w_down)
    slope = (
        0.5 * (1.0 + lax.erf(pre_act * 0.7071067811865476))
        + pre_act * jnp.exp(-0.5 * pre_act * pre_act) * 0.3989422804014327
    )
    grad_pre = (grad_hidden * slope).astype(jnp.bfloat16)
    grad_up = product("bld,blf->df", ff_input, grad_pre)
    grad_norm_ff = product("blf,df->bld", grad_pre, w_up)
    grad_mixed_norm, grad_ff_gain, grad_ff_bias = norm_back(
        grad_norm_ff, ff_hat, ff_factor, ff_gain
    )
    grad_mixed = upstream + grad_mixed_norm
    mixed_low = grad_mixed.astype(jnp.bfloat16)
    grad_out = product("ble,bld->ed", attended, mixed_low)
    grad_attended = split_heads(product("bld,ed->ble", mixed_low, w_out).astype(jnp.bfloat16))
    query_heads = split_heads(query)
    key_heads = split_heads(keyval[..., :inner_width])
    value_heads = split_heads(keyval[..., inner_width:])
    scores = product("blhe,bnhe->bhln", query_heads, key_heads)
    attn_prob = jnp.exp(scores - log_total)
    grad_value = product("bhln,blhe->bnhe", attn_prob.astype(jnp.bfloat16), grad_attended).astype(
        jnp.bfloat16
    )
    grad_prob = product("blhe,bnhe->bhln", grad_attended, value_heads)
    grad_scores = (
        attn_prob * (grad_prob - jnp.sum(attn_prob * grad_prob, axis=-1, keepdims=True))
    ).astype(jnp.bfloat16)
    grad_query_low = product("bhln,bnhe->blhe", grad_scores, key_heads).astype(
        jnp.bfloat16
    ).reshape(query.shape) * HEAD_DIM ** (-0.5)
    grad_key = product("bhln,blhe->bnhe", grad_scores, query_heads).astype(jnp.bfloat16)
    batch_rows = (grad_key.shape[0], grad_key.shape[1], inner_width)
    grad_keyval = jnp.concatenate(
        [grad_key.reshape(batch_rows), grad_value.reshape(batch_rows)], axis=-1
    )
    grad_wq = product("bld,ble->de", joined[:, patch_rows:], grad_query_low)
    grad_latent_norm = product("ble,de->bld", grad_query_low, w_query)
    grad_wkv = product("bnd,bne->de", joined, grad_keyval)
    grad_joined = product("bne,de->bnd", grad_keyval, w_kv)
    grad_latent_norm = grad_latent_norm + grad_joined[:, patch_rows:]
    grad_media, grad_media_gain, grad_media_bias = norm_back(
        grad_joined[:, :patch_rows], media_hat, media_factor, media_gain
    )
    grad_latent_part, grad_latent_gain, grad_latent_bias = norm_back(
        grad_latent_norm, latent_hat, latent_factor, latent_gain
    )
    grads = (
        grad_media_gain,
        grad_media_bias,
        grad_latent_gain,
        grad_latent_bias,
        grad_wq,
        grad_wkv,
        grad_out,
        grad_ff_gain,
        grad_ff_bias,
        grad_up,
        grad_down,
    )
    return (grad_mixed + grad_latent_part, grad_media, grads)


def put_rows(buffer, values, start, is_valid):
    former = lax.dynamic_slice_in_dim(buffer, start, values.shape[0], 0)
    return lax.dynamic_update_slice_in_dim(buffer, jnp.where(is_valid, values, former), start, 0)


def put_slot(buffer, values, slot_index, is_valid):
    return put_rows(buffer, values[None], slot_index, is_valid)


def shards(
    media,
    image_live,
    start_latents,
    latent_cotangent,
    media_gain,
    media_bias,
    latent_gain,
    latent_bias,
    w_query,
    w_kv,
    w_out,
    ff_gain,
    ff_bias,
    w_up,
    w_down,
):
    params = (
        media_gain[0],
        media_bias[0],
        latent_gain[0],
        latent_bias[0],
        w_query[0],
        w_kv[0],
        w_out[0],
        ff_gain[0],
        ff_bias[0],
        w_up[0],
        w_down[0],
    )
    micro_count = MB
    group_size = media.shape[0] // micro_count
    latent_rows, feature_dim = start_latents.shape
    patch_rows = media.shape[1]
    section_index = lax.axis_index("section")
    first_section = section_index == 0
    begin = jnp.broadcast_to(
        start_latents.astype(jnp.float32), (group_size, latent_rows, feature_dim)
    )
    received = jnp.zeros((group_size, latent_rows, feature_dim), jnp.bfloat16)
    outputs = jnp.zeros((media.shape[0], latent_rows, feature_dim), jnp.bfloat16)
    stored = None
    for tick_index in range(micro_count + 1):
        micro_index = tick_index - section_index
        is_valid = (micro_index >= 0) & (micro_index < micro_count)
        slot_index = jnp.clip(micro_index, 0, micro_count - 1)
        media_rows = lax.dynamic_slice_in_dim(media, slot_index * group_size, group_size, 0)
        inputs = jnp.where(first_section, begin, received.astype(jnp.float32))
        result, kept = layer_forward(inputs, media_rows, params)
        sent = result.astype(jnp.bfloat16)
        outputs = put_rows(outputs, sent, slot_index * group_size, is_valid)
        if stored is None:
            stored = jax.tree.map(
                lambda entry: jnp.zeros((micro_count,) + entry.shape, entry.dtype), kept
            )
        stored = jax.tree.map(
            lambda buffer, entry: put_slot(buffer, entry, slot_index, is_valid), stored, kept
        )
        if tick_index < micro_count:
            received = shifted(sent, "section", 1)
    totals = tuple((jnp.zeros((1,) + entry.shape, jnp.float32) for entry in params)) + (
        jnp.zeros((latent_rows, feature_dim), jnp.float32),
    )
    shard_totals = None
    media_total = jnp.zeros((media.shape[0], patch_rows, feature_dim), jnp.float32)
    back_received = jnp.zeros((group_size, latent_rows, feature_dim), jnp.bfloat16)
    for tick_index in range(micro_count + 1):
        micro_index = tick_index + section_index - 1
        is_valid = (micro_index >= 0) & (micro_index < micro_count)
        slot_index = jnp.clip(micro_index, 0, micro_count - 1)
        live_rows = lax.dynamic_slice_in_dim(
            image_live, slot_index * group_size, group_size, 0
        ).astype(jnp.float32)
        target = (
            lax.dynamic_slice_in_dim(
                latent_cotangent, slot_index * group_size, group_size, 0
            ).astype(jnp.float32)
            * live_rows[:, None, None]
        )
        upstream = jnp.where(first_section, back_received.astype(jnp.float32), target)
        kept = jax.tree.map(
            lambda buffer: lax.dynamic_index_in_dim(buffer, slot_index, 0, keepdims=False), stored
        )
        grad_latent, grad_media, grads = layer_backward(kept, upstream, params)
        media_total = put_rows(media_total, grad_media, slot_index * group_size, is_valid)
        start_term = jnp.where(first_section & is_valid, jnp.sum(grad_latent, axis=0), 0.0)
        terms = tuple((jnp.where(is_valid, entry[None], 0.0) for entry in grads)) + (start_term,)
        totals = tuple((total + term for total, term in zip(totals, terms)))
        if tick_index < micro_count:
            back_received = shifted(grad_latent.astype(jnp.bfloat16), "section", -1)
    shard_totals = lax.psum_scatter(totals, "dp", scatter_dimension=1, tiled=True)
    media_grad = lax.psum_scatter(
        media_total.astype(jnp.bfloat16), "section", scatter_dimension=2, tiled=True
    ).astype(jnp.float32)
    start_grad = lax.psum_scatter(shard_totals[-1], "section", scatter_dimension=0, tiled=True)
    return (outputs[None], media_grad, start_grad) + tuple(shard_totals[:-1])


def solution(mesh):
    in_specs = (
        P("dp", None, None),
        P("dp"),
        P(),
        P("dp", None, None),
        P("section", None),
        P("section", None),
        P("section", None),
        P("section", None),
        P("section", None, None),
        P("section", None, None),
        P("section", None, None),
        P("section", None),
        P("section", None),
        P("section", None, None),
        P("section", None, None),
    )
    out_specs = (
        P("section", "dp", None, None),
        P("dp", None, "section"),
        P("section", "dp"),
        P("section", "dp"),
        P("section", "dp"),
        P("section", "dp"),
        P("section", "dp"),
        P("section", "dp", None),
        P("section", "dp", None),
        P("section", "dp", None),
        P("section", "dp"),
        P("section", "dp"),
        P("section", "dp", None),
        P("section", "dp", None),
    )
    return jax.shard_map(shards, mesh=mesh, in_specs=in_specs, out_specs=out_specs, check_vma=False)
```

profile of v0, /device:TPU:10, one launch (start us, length us, event | category | flops | bytes accessed | tf_op | source)
XLA Modules:
  0.0 2059.1 jit_solution(7123254296972423390)
XLA Ops:
  22.8 5.4 fusion.122
  43.9 6.1 fusion.488
  51.4 4.9 bitcast_dynamic-update-slice_fusion.2
  123.5 5.7 fusion.489
  131.2 7.3 fusion.372
  170.3 6.1 fusion.490
  178.4 7.0 fusion.371
  217.3 5.7 fusion.491
  225.0 7.1 fusion.370
  251.7 4.8 fusion.307
  256.5 5.5 dynamic-slice_bitcast_fusion.5
  284.4 6.6 fusion.492
  294.9 5.0 fusion.77
  341.9 7.2 fusion.74
  349.1 7.4 fusion.451
  393.8 7.2 fusion.71
  401.1 7.4 fusion.441
  441.0 7.2 fusion.68
  448.3 7.4 fusion.431
  490.2 7.2 fusion.65
  497.5 7.4 fusion.421
  528.0 8.5 slice_reduce_fusion
  584.2 13.9 reduce-scatter.43.cloned.1.call-done
  599.6 5.0 fusion.166
  629.1 5.0 fusion.81
  636.8 8.1 fusion.513
  644.9 8.1 fusion.511
  653.0 8.1 fusion.509
  661.1 8.1 fusion.507
  669.3 28.6 %fusion.6 = f32[1,1024,4096]{2,1,0:T(8,128)} fusion(f32[1024,4096,1]{1,0,2:T(8,128)} %fusion.507, f32[1024,4096,1]{1,0,2:T(8,128)} %fusion.509, f32[1024,4096,1]{1,0,2:T(8,128)} %fusion.511, f32[1024,4096,1]{1,0,2:T(8,128)} %fusion.513, bf16[2,64,4096]{2,1,0:T(8,128)(2,1)S(1)} %copy-done.78, pred[]{:T(512)S(6)} %and.55, pred[]{:T(512)S(6)} %and.54, ...), kind=kOutput, calls=%fused_computation.12 | convolution fusion | flops 1111490560 | bytes 85196808 | tf_op jit(solution)/shard_map/bld,blf->df/dot_general | solution.py:18
  699.5 7.1 fusion.369
  706.7 9.5 fusion.367
  716.2 9.1 fusion.365
  725.3 9.1 fusion.363
  734.5 9.2 fusion.361
  743.7 29.3 %fusion.1 = f32[1,4096,1024]{2,1,0:T(8,128)} fusion(f32[4096,1024,1]{1,0,2:T(8,128)} %fusion.361, f32[4096,1024,1]{1,0,2:T(8,128)} %fusion.363, f32[4096,1024,1]{1,0,2:T(8,128)} %fusion.365, f32[4096,1024,1]{1,0,2:T(8,128)} %fusion.367, pred[]{:T(512)S(6)} %and.55, pred[]{:T(512)S(6)} %and.54, pred[]{:T(512)S(6)} %and.53, pred[]{:T(512)S(6)} %and.52, ...), kind=kOutput, calls=%fused_computation.2 | convolution fusion | flops 1112145920 | bytes 85458968 | tf_op jit(solution)/shard_map/blf,bld->fd/dot_general | solution.py:18
  775.2 5.4 fusion.357
  783.3 40.5 %reduce-scatter.49.cloned.1.call-done = f32[64,1]{1,0:T(8,128)} async-done(((f32[1024,1]{1,0:T(8,128)}), f32[64,1]{1,0:T(8,128)}) %reduce-scatter.49.cloned.1.call-update) | async-done | bytes 272
  825.1 73.7 %reduce-scatter.51.cloned.1.call-done = f32[64,1]{1,0:T(8,128)} async-done(((f32[1024,1]{1,0:T(8,128)}), f32[64,1]{1,0:T(8,128)}) %reduce-scatter.51.cloned.1.call-update) | async-done | bytes 272
  900.2 73.7 %reduce-scatter.45.cloned.1.call-done = f32[64,1]{1,0:T(8,128)} async-done(((f32[1024,1]{1,0:T(8,128)}), f32[64,1]{1,0:T(8,128)}) %reduce-scatter.45.cloned.1.call-update) | async-done | bytes 272
  975.2 73.9 %reduce-scatter.47.cloned.1.call-done = f32[64,1]{1,0:T(8,128)} async-done(((f32[1024,1]{1,0:T(8,128)}), f32[64,1]{1,0:T(8,128)}) %reduce-scatter.47.cloned.1.call-update) | async-done | bytes 272
  1050.6 20.5 reduce-scatter.29.cloned.1.call-done
  1075.3 7.2 reduce-scatter.31.cloned.1.call-done
  1082.5 74.6 %reduce-scatter.37.cloned.1.call-done = f32[1,32,1024]{2,1,0:T(8,128)} async-done(((f32[1,512,1024]{2,1,0:T(8,128)}), f32[1,32,1024]{2,1,0:T(8,128)}) %reduce-scatter.37.cloned.1.call-update) | async-done | bytes 131088 | tf_op jit(solution)/shard_map/reduce_scatter | solution.py:295
  1157.1 81.6 %reduce-scatter.33.cloned.1.call-done = f32[1,64,512]{2,1,0:T(8,128)} async-done(((f32[1,1024,512]{2,1,0:T(8,128)}), f32[1,64,512]{2,1,0:T(8,128)}) %reduce-scatter.33.cloned.1.call-update) | async-done | bytes 131088 | tf_op jit(solution)/shard_map/reduce_scatter | solution.py:295
  1238.7 103.7 %reduce-scatter.35.cloned.1.call-done = f32[1,64,1024]{2,1,0:T(8,128)} async-done(((f32[1,1024,1024]{2,1,0:T(8,128)}), f32[1,64,1024]{2,1,0:T(8,128)}) %reduce-scatter.35.cloned.1.call-update) | async-done | bytes 262160 | tf_op jit(solution)/shard_map/reduce_scatter | solution.py:295
  1342.4 354.9 %reduce-scatter.39.cloned.1.call-done = f32[1,64,4096]{2,1,0:T(8,128)} async-done(((f32[1,1024,4096]{2,1,0:T(8,128)}), f32[1,64,4096]{2,1,0:T(8,128)}) %reduce-scatter.39.cloned.1.call-update) | async-done | bytes 1048592 | tf_op jit(solution)/shard_map/reduce_scatter | solution.py:295
  1697.3 354.8 %reduce-scatter.41.cloned.1.call-done = f32[1,256,1024]{2,1,0:T(8,128)} async-done(((f32[1,4096,1024]{2,1,0:T(8,128)}), f32[1,256,1024]{2,1,0:T(8,128)}) %reduce-scatter.41.cloned.1.call-update) | async-done | bytes 1048592 | tf_op jit(solution)/shard_map/reduce_scatter | solution.py:295
  (1002 shorter events, 474.0 us)
Async XLA Ops:
  7.2 24.0 %copy-start = (bf16[1,1024,1024]{2,1,0:T(8,128)(2,1)S(1)}, bf16[1,1024,1024]{2,1,0:T(8,128)(2,1)}, u32[]{:S(2)}) copy-start(bf16[1,1024,1024]{2,1,0:T(8,128)(2,1)} %param.24) | copy-start | bytes 6291460
  7.2 590.9 %reduce-scatter.43.cloned.1.call-start = ((), (), s32[]{:S(2)}) async-start(), calls=%async_computation.21 | async-start | bytes 557056
  10.7 12.1 copy-start.173
  16.3 57.8 %copy-start.30 = (f32[64,1024]{1,0:T(8,128)}, f32[64,1024]{1,0:T(8,128)S(1)}, u32[]{:S(2)}) copy-start(f32[64,1024]{1,0:T(8,128)S(1)} %get-tuple-element.177) | copy-start | bytes 786436
  43.2 13.3 slice-start.2
  43.6 12.9 copy-start.24
  43.9 12.6 slice-start.3
  59.5 39.1 %collective-permute-start = (bf16[2,64,1024]{2,1,0:T(8,128)(2,1)}, bf16[2,64,1024]{2,1,0:T(8,128)(2,1)}, u32[]{:S(2)}, u32[]{:S(2)}) collective-permute-start(bf16[2,64,1024]{2,1,0:T(8,128)(2,1)} %get-tuple-element.210), channel_id=1, source_target_pairs={{0,16},{1,17},{2,18},{3,19},{4,20},{5,21},{6,22},{7,23},{8,24},{9,... | collective-permute-start | bytes 786440 | tf_op jit(solution)/shard_map/ppermute | solution.py:14
  64.1 10.9 copy-start.171
  64.1 10.9 copy-start.184
  64.1 11.5 copy-start.254
  121.7 16.8 slice-start.4
  123.2 15.3 copy-start.18
  123.5 15.0 slice-start.5
  141.5 7.9 collective-permute-start.1
  169.7 15.8 slice-start.6
  170.1 15.4 copy-start.20
  170.3 15.1 slice-start.7
  188.5 7.8 collective-permute-start.2
  215.3 16.7 slice-start.8
  217.0 15.1 copy-start.22
  217.3 14.8 slice-start.9
  235.1 7.9 collective-permute-start.3
  278.7 16.2 slice-start.10
  281.4 18.5 copy-start.16
  281.4 18.5 copy-start.211
  281.7 18.2 copy-start.240
  290.9 11.9 slice-start
  334.3 7.6 collective-permute-start.4
  381.3 12.5 collective-permute-start.5
  433.2 7.8 collective-permute-start.6
  480.4 9.8 collective-permute-start.7
  527.7 252.9 %reduce-scatter.53.cloned.1.call-start = ((), (), s32[]{:S(2)}) async-start(), calls=%async_computation.26 | async-start | bytes 557056
  537.8 244.2 %reduce-scatter.55.cloned.1.call-start = ((), (), s32[]{:S(2)}) async-start(), calls=%async_computation.27 | async-start | bytes 557056
  539.0 284.8 %reduce-scatter.49.cloned.1.call-start = ((), (), s32[]{:S(2)}) async-start(), calls=%async_computation.24 | async-start | bytes 557056
  540.1 358.7 %reduce-scatter.51.cloned.1.call-start = ((), (), s32[]{:S(2)}) async-start(), calls=%async_computation.25 | async-start | bytes 557056
  541.3 432.6 %reduce-scatter.45.cloned.1.call-start = ((), (), s32[]{:S(2)}) async-start(), calls=%async_computation.22 | async-start | bytes 557056
  542.5 506.7 %reduce-scatter.47.cloned.1.call-start = ((), (), s32[]{:S(2)}) async-start(), calls=%async_computation.23 | async-start | bytes 557056
  543.6 527.6 %reduce-scatter.29.cloned.1.call-start = ((), (), s32[]{:S(2)}) async-start(), calls=%async_computation.14 | async-start | bytes 6291456 | tf_op jit(solution)/shard_map/reduce_scatter | solution.py:296
  565.0 517.5 %reduce-scatter.31.cloned.1.call-start = ((), (), s32[]{:S(2)}) async-start(), calls=%async_computation.15 | async-start | bytes 49152 | tf_op jit(solution)/shard_map/reduce_scatter | solution.py:299
  581.4 18.2 copy-start.51
  599.6 557.6 %reduce-scatter.37.cloned.1.call-start = ((), (), s32[]{:S(2)}) async-start(), calls=%async_computation.18 | async-start | bytes 2228224 | tf_op jit(solution)/shard_map/reduce_scatter | solution.py:295
  604.7 634.1 %reduce-scatter.33.cloned.1.call-start = ((), (), s32[]{:S(2)}) async-start(), calls=%async_computation.16 | async-start | bytes 2228224 | tf_op jit(solution)/shard_map/reduce_scatter | solution.py:295
  618.8 723.6 %reduce-scatter.35.cloned.1.call-start = ((), (), s32[]{:S(2)}) async-start(), calls=%async_computation.17 | async-start | bytes 4456448 | tf_op jit(solution)/shard_map/reduce_scatter | solution.py:295
  634.3 1063.0 %reduce-scatter.39.cloned.1.call-start = ((), (), s32[]{:S(2)}) async-start(), calls=%async_computation.19 | async-start | bytes 17825792 | tf_op jit(solution)/shard_map/reduce_scatter | solution.py:295
  636.8 24.3 %copy-start.27 = (bf16[4,2,64,1024]{3,2,1,0:T(8,128)(2,1)}, bf16[4,2,64,1024]{3,2,1,0:T(8,128)(2,1)S(1)}, u32[]{:S(2)}) copy-start(bf16[4,2,64,1024]{3,2,1,0:T(8,128)(2,1)S(1)} %fusion.515) | copy-start | bytes 3145732
  697.9 1354.1 %reduce-scatter.41.cloned.1.call-start = ((), (), s32[]{:S(2)}) async-start(), calls=%async_computation.20 | async-start | bytes 17825792 | tf_op jit(solution)/shard_map/reduce_scatter | solution.py:295
  1049.1 1002.9 %copy-start.1 = (bf16[1,1024,1024]{2,1,0:T(8,128)(2,1)S(1)}, bf16[1,1024,1024]{2,1,0:T(8,128)(2,1)}, u32[]{:S(2)}) copy-start(bf16[1,1024,1024]{2,1,0:T(8,128)(2,1)} %param.24) | copy-start | bytes 6291460
  (275 other events, 1014.5 us)
Sparse Core Ops, SparseCore 0:
  527.7 70.3 reduce-scatter.42
  600.4 72.9 reduce-scatter.52
  675.7 72.9 reduce-scatter.54
  750.8 72.9 reduce-scatter.48
  825.9 72.8 reduce-scatter.50
  901.0 72.8 reduce-scatter.44
  976.1 72.9 reduce-scatter.46
  1051.5 19.5 reduce-scatter.28
  1073.9 8.5 reduce-scatter.30
  1085.2 71.8 reduce-scatter.36
  1160.0 78.7 reduce-scatter.32
  1241.5 100.8 reduce-scatter.34
  1345.3 351.9 reduce-scatter.38
  1700.0 351.9 reduce-scatter.40
where the time goes:
time: 2070 us; the launch traced here: 2060 us
  waiting for transfers between devices  1270 us (61%)
  matrix products  384 us (19%)
  other arithmetic  190 us (9%)
  local copies, waits for them, and re-layouts  180 us (9%)
    reduce_scatter x5, waiting for transfers between devices, shards(): lax.psum_scatter(totals, 'dp', scatter_dimension=1, tiled=True)  970 us
    dot_general x110, matrix products, product(): return jnp.einsum(form, left, right, preferred_element_type=jnp.float32)  384 us
    unnamed x21, waiting for transfers between devices  276 us
    dynamic_update_slice x62, other arithmetic, put_rows(): lax.dynamic_update_slice_in_dim(buffer, jnp.where(is_valid, values, forme...  131 us
    unnamed x617, local copies, waits for them, and re-layouts  44.1 us
  transfers between devices with their start and end apart: 22, of which 12 were waited for; matrix products, arithmetic and copies ran while one was open for 16% of the time, Pallas kernels for 0%

commit v1 on v0

v1 whole, which is shorter than its diff:
```python
import functools

import jax
import jax.numpy as jnp
from jax import lax
from jax.experimental import pallas as pl
from jax.experimental.pallas import tpu as pltpu
from jax.sharding import PartitionSpec as P

MESH = pl.DeviceIdType.MESH
F32 = jnp.float32
BF16 = jnp.bfloat16
HEAD_DIM = 64
LANES = 256
GROUP = 4


def dot(left, right):
    return jnp.dot(left, right, preferred_element_type=F32)


def dot_rows(left, right):
    return lax.dot_general(left, right, (((1,), (1,)), ((), ())), preferred_element_type=F32)


def dot_cols(left, right):
    return lax.dot_general(left, right, (((0,), (0,)), ((), ())), preferred_element_type=F32)


def normed(value):
    centred = value - jnp.mean(value, axis=-1, keepdims=True)
    factor = lax.rsqrt(jnp.mean(centred * centred, axis=-1, keepdims=True) + 1e-05)
    return centred * factor, factor


def norm_back(upstream, hat, factor, gain):
    scaled = upstream * gain
    return factor * (
        scaled
        - jnp.mean(scaled, axis=-1, keepdims=True)
        - hat * jnp.mean(scaled * hat, axis=-1, keepdims=True)
    )


def gelu_and_slope(u):
    e = jnp.exp(-0.5 * (u * u))
    d = 1.0 + jnp.abs(u) * (0.3275911 * 0.7071067811865476)
    t = pl.reciprocal(d, approx=True)
    t = t * (2.0 - d * t)
    tail = t * (
        0.127414796 + t * (-0.142248368 + t * (0.7107068705 + t * (-0.7265760135 + t * 0.5307027145)))
    )
    tail = tail * e
    phi = jnp.where(u >= 0.0, 1.0 - tail, tail)
    return u * phi, phi + (u * e) * 0.3989422804014327


def layer_kernel(
    dims,
    start,
    media,
    g_in,
    vectors,
    wq,
    wkv,
    wo,
    wu,
    wd,
    y_out,
    j_out,
    o_out,
    f_out,
    h_out,
    du_out,
    dz1_out,
    dq_out,
    dkv_out,
    g_out,
    sums,
    start_sum,
    wq_v,
    wkv_v,
    wo_v,
    wu_v,
    wd_v,
    j_v,
    kv_v,
    z_v,
    q_v,
    p_v,
    o_v,
    z1_v,
    f_v,
    h_v,
    sl_v,
    y_v,
    acc,
    g_v,
    dz1_v,
    dq_v,
    do_v,
    dz_v,
    mask_v,
    load_sem,
    store_sem,
    send_sem,
    recv_sem,
):
    images, latents, patches, inner, hidden, step = dims
    rows = images * latents
    per = GROUP * latents
    batches = images // GROUP
    groups = inner // LANES
    heads = LANES // HEAD_DIM
    chunks = hidden // step
    section = lax.axis_index("section")
    dp = lax.axis_index("dp")
    sibling = (1 - section, dp)

    def load(k, src, dst):
        return pltpu.make_async_copy(src, dst, load_sem.at[k])

    loads = [
        load(0, wkv, wkv_v),
        load(1, wq, wq_v),
        load(2, wo, wo_v),
        load(3, wu, wu_v),
        load(4, wd, wd_v),
    ]

    def media_load(i):
        return load(6 + i, media.at[i], j_v.at[i, pl.ds(0, patches)])

    media_load(0).start()
    loads[0].start()
    for i in range(1, images):
        media_load(i).start()
    for copy in loads[1:]:
        copy.start()
    g_load = load(5, g_in, g_v)

    def start_load(i):
        return load(6 + images + i, start, z_v.at[pl.ds(i * latents, latents)])

    @pl.when(section == 0)
    def _():
        for i in range(images):
            start_load(i).start()

    @pl.when(section == 1)
    def _():
        g_load.start()

    barrier = pltpu.get_barrier_semaphore()
    pl.semaphore_signal(barrier, inc=1, device_id=sibling, device_id_type=MESH)

    row_head = lax.broadcasted_iota(jnp.int32, (heads * latents, LANES), 0) // latents
    lane_head = lax.broadcasted_iota(jnp.int32, (heads * latents, LANES), 1) // HEAD_DIM
    mask_v[...] = jnp.where(row_head == lane_head, 1.0, 0.0).astype(F32)
    sums[...] = jnp.zeros_like(sums)
    start_sum[...] = jnp.zeros_like(start_sum)

    loads[0].wait()

    def media_step(i, carry):
        media_load(i).wait()
        hat, _ = normed(j_v[i, pl.ds(0, patches), :].astype(F32))
        low = (hat * vectors[0:1, :] + vectors[1:2, :]).astype(BF16)
        j_v[i, pl.ds(0, patches), :] = low
        kv_v[i, pl.ds(0, patches), :] = dot(low, wkv_v[...]).astype(BF16)
        return carry

    lax.fori_loop(0, images, media_step, 0)
    for copy in loads[1:]:
        copy.wait()

    @pl.when(section == 0)
    def _():
        for i in range(images):
            start_load(i).wait()

    @pl.when(section == 1)
    def _():
        g_load.wait()

    pl.semaphore_wait(barrier, 1)

    def relay_latents(b):
        span = pl.ds(b * per, per)
        return pltpu.make_async_remote_copy(
            src_ref=y_v.at[span],
            dst_ref=z_v.at[span],
            send_sem=send_sem.at[b],
            recv_sem=recv_sem.at[b],
            device_id=sibling,
            device_id_type=MESH,
        )

    def relay_grad(b):
        span = pl.ds(b * per, per)
        return pltpu.make_async_remote_copy(
            src_ref=dz_v.at[span],
            dst_ref=g_v.at[span],
            send_sem=send_sem.at[batches + b],
            recv_sem=recv_sem.at[batches + b],
            device_id=sibling,
            device_id_type=MESH,
        )

    def spread(block):
        return (jnp.concatenate([block] * heads, axis=0).astype(F32) * mask_v[...]).astype(BF16)

    def gathered(block):
        kept = block * mask_v[...]
        total = kept[0:latents]
        for k in range(1, heads):
            total = total + kept[k * latents : (k + 1) * latents]
        return total

    def forward(b, carry):
        first = pl.multiple_of(b * per, per)
        span = pl.ds(first, per)

        @pl.when(section == 1)
        def _():
            relay_latents(b).wait_recv()

        z = z_v[span, :].astype(F32)
        hat, _ = normed(z)
        low = (hat * vectors[2:3, :] + vectors[3:4, :]).astype(BF16)
        j_v[pl.ds(b * GROUP, GROUP), pl.ds(patches, latents), :] = low.reshape(GROUP, latents, -1)
        q_v[span, :] = (dot(low, wq_v[...]) * HEAD_DIM**-0.5).astype(BF16)
        kv_v[pl.ds(b * GROUP, GROUP), pl.ds(patches, latents), :] = (
            dot(low, wkv_v[...]).astype(BF16).reshape(GROUP, latents, -1)
        )

        def attend(k, inner_carry):
            i = b * GROUP + k
            mine = pl.ds(pl.multiple_of(i * latents, latents), latents)
            for g in range(groups):
                lanes = slice(g * LANES, (g + 1) * LANES)
                values = slice(inner + g * LANES, inner + (g + 1) * LANES)
                scores = dot_rows(spread(q_v[mine, lanes]), kv_v[i, :, lanes])
                e = jnp.exp(scores - jnp.max(scores, axis=-1, keepdims=True))
                prob = (e / jnp.sum(e, axis=-1, keepdims=True)).astype(BF16)
                p_v[i * groups + g] = prob
                o_v[mine, lanes] = gathered(dot(prob, kv_v[i, :, values])).astype(BF16)
            return inner_carry

        lax.fori_loop(0, GROUP, attend, 0)
        mixed = z + dot(o_v[span, :], wo_v[...])
        z1_v[span, :] = mixed
        hat, _ = normed(mixed)
        low = (hat * vectors[4:5, :] + vectors[5:6, :]).astype(BF16)
        f_v[span, :] = low
        u = dot(low, wu_v[:, 0:step])
        for c in range(chunks):
            lanes = slice(c * step, (c + 1) * step)
            if c + 1 < chunks:
                later = dot(low, wu_v[:, (c + 1) * step : (c + 2) * step])
            h, slope = gelu_and_slope(u)
            h = h.astype(BF16)
            h_v[span, lanes] = h
            sl_v[span, lanes] = slope.astype(BF16)
            part = dot(h, wd_v[lanes, :])
            acc[...] = part + (mixed if c == 0 else acc[...])
            u = later
        y_v[span, :] = acc[...].astype(BF16)

        @pl.when(section == 0)
        def _():
            relay_latents(b).start()

        return carry

    lax.fori_loop(0, batches, forward, 0)

    def store(k, src, dst):
        return pltpu.make_async_copy(src, dst, store_sem.at[k])

    stores = [
        store(0, y_v, y_out),
        store(1, j_v, j_out),
        store(2, o_v, o_out),
        store(3, f_v, f_out),
        store(4, h_v, h_out),
    ]
    for copy in stores:
        copy.start()

    def backward(b, carry):
        first = pl.multiple_of(b * per, per)
        span = pl.ds(first, per)

        @pl.when(section == 0)
        def _():
            relay_grad(b).wait_recv()

        g = g_v[span, :]
        dh = dot_rows(g, wd_v[0:step, :])
        for c in range(chunks):
            lanes = slice(c * step, (c + 1) * step)
            if c + 1 < chunks:
                later = dot_rows(g, wd_v[(c + 1) * step : (c + 2) * step, :])
            du = (dh * sl_v[span, lanes].astype(F32)).astype(BF16)
            sl_v[span, lanes] = du
            part = dot_rows(du, wu_v[:, lanes])
            acc[...] = part if c == 0 else acc[...] + part
            dh = later
        df = acc[...]
        hat, factor = normed(z1_v[span, :])
        sums[4:5, :] += jnp.sum(df * hat, axis=0, keepdims=True)
        sums[5:6, :] += jnp.sum(df, axis=0, keepdims=True)
        dz1 = g.astype(F32) + norm_back(df, hat, factor, vectors[4:5, :])
        z1_v[span, :] = dz1
        low = dz1.astype(BF16)
        dz1_v[span, :] = low
        do_v[...] = dot_rows(low, wo_v[...]).astype(BF16)

        def attend(k, inner_carry):
            i = b * GROUP + k
            mine = pl.ds(pl.multiple_of(i * latents, latents), latents)
            local = pl.ds(pl.multiple_of(k * latents, latents), latents)
            for n in range(groups):
                lanes = slice(n * LANES, (n + 1) * LANES)
                values = slice(inner + n * LANES, inner + (n + 1) * LANES)
                prob = p_v[i * groups + n]
                wide = spread(do_v[local, lanes])
                keys = kv_v[i, :, lanes]
                dv = dot_cols(prob, wide)
                dp_ = dot_rows(wide, kv_v[i, :, values])
                pf = prob.astype(F32)
                ds = (pf * (dp_ - jnp.sum(pf * dp_, axis=-1, keepdims=True))).astype(BF16)
                dk = dot_cols(ds, spread(q_v[mine, lanes]))
                dq = gathered(dot(ds, keys)).astype(BF16)
                dq_v[mine, lanes] = dq * BF16(HEAD_DIM**-0.5)
                kv_v[i, :, lanes] = dk.astype(BF16)
                kv_v[i, :, values] = dv.astype(BF16)
            return inner_carry

        lax.fori_loop(0, GROUP, attend, 0)
        tail = kv_v[pl.ds(b * GROUP, GROUP), pl.ds(patches, latents), :].reshape(per, -1)
        dn = dot_rows(dq_v[span, :], wq_v[...]) + dot_rows(tail, wkv_v[...])
        hat, factor = normed(z_v[span, :].astype(F32))
        sums[2:3, :] += jnp.sum(dn * hat, axis=0, keepdims=True)
        sums[3:4, :] += jnp.sum(dn, axis=0, keepdims=True)
        dz = z1_v[span, :] + norm_back(dn, hat, factor, vectors[2:3, :])
        dz_v[span, :] = dz.astype(BF16)

        @pl.when(section == 1)
        def _():
            relay_grad(b).start()

        @pl.when(section == 0)
        def _():
            total = dz[0:latents]
            for k in range(1, GROUP):
                total = total + dz[k * latents : (k + 1) * latents]
            start_sum[...] += total

        return carry

    lax.fori_loop(0, batches, backward, 0)
    late = [
        store(5, sl_v, du_out),
        store(6, dz1_v, dz1_out),
        store(7, dq_v, dq_out),
        store(8, kv_v, dkv_out),
        store(9, g_v, g_out),
    ]
    for copy in late:
        copy.start()
    for copy in stores + late:
        copy.wait()

    @pl.when(section == 0)
    def _():
        for b in range(batches):
            relay_latents(b).wait_send()

    @pl.when(section == 1)
    def _():
        for b in range(batches):
            relay_grad(b).wait_send()


def layers(start, media, g_in, vectors, wq, wkv, wo, wu, wd, collective_id=2):
    images, patches, width = media.shape
    latents = start.shape[0]
    inner = wq.shape[1]
    hidden = wu.shape[1]
    rows = images * latents
    per = GROUP * latents
    batches = images // GROUP
    groups = inner // LANES
    step = 512
    dims = (images, latents, patches, inner, hidden, step)
    any_spec = pl.BlockSpec(memory_space=pl.ANY)
    vmem_spec = pl.BlockSpec(memory_space=pltpu.VMEM)
    keys = patches + latents

    def low(*shape):
        return jax.ShapeDtypeStruct(shape, BF16)

    out_shape = [
        low(rows, width),
        low(images, keys, width),
        low(rows, inner),
        low(rows, width),
        low(rows, hidden),
        low(rows, hidden),
        low(rows, width),
        low(rows, inner),
        low(images, keys, 2 * inner),
        low(rows, width),
        jax.ShapeDtypeStruct((8, width), F32),
        jax.ShapeDtypeStruct((latents, width), F32),
    ]
    scratch = [
        pltpu.VMEM(wq.shape, BF16),
        pltpu.VMEM(wkv.shape, BF16),
        pltpu.VMEM(wo.shape, BF16),
        pltpu.VMEM(wu.shape, BF16),
        pltpu.VMEM(wd.shape, BF16),
        pltpu.VMEM((images, keys, width), BF16),
        pltpu.VMEM((images, keys, 2 * inner), BF16),
        pltpu.VMEM((rows, width), BF16),
        pltpu.VMEM((rows, inner), BF16),
        pltpu.VMEM((images * groups, LANES // HEAD_DIM * latents, keys), BF16),
        pltpu.VMEM((rows, inner), BF16),
        pltpu.VMEM((rows, width), F32),
        pltpu.VMEM((rows, width), BF16),
        pltpu.VMEM((rows, hidden), BF16),
        pltpu.VMEM((rows, hidden), BF16),
        pltpu.VMEM((rows, width), BF16),
        pltpu.VMEM((per, width), F32),
        pltpu.VMEM((rows, width), BF16),
        pltpu.VMEM((rows, width), BF16),
        pltpu.VMEM((rows, inner), BF16),
        pltpu.VMEM((per, inner), BF16),
        pltpu.VMEM((rows, width), BF16),
        pltpu.VMEM((LANES // HEAD_DIM * latents, LANES), F32),
        pltpu.SemaphoreType.DMA((6 + 2 * images,)),
        pltpu.SemaphoreType.DMA((10,)),
        pltpu.SemaphoreType.DMA((2 * batches,)),
        pltpu.SemaphoreType.DMA((2 * batches,)),
    ]
    return pl.pallas_call(
        functools.partial(layer_kernel, dims),
        out_shape=out_shape,
        in_specs=[any_spec] * 3 + [vmem_spec] + [any_spec] * 5,
        out_specs=[any_spec] * 10 + [vmem_spec] * 2,
        scratch_shapes=scratch,
        compiler_params=pltpu.CompilerParams(
            collective_id=collective_id, has_side_effects=True, vmem_limit_bytes=62 * 1024 * 1024
        ),
        name="layers",
    )(start, media, g_in, vectors, wq, wkv, wo, wu, wd)


def rs_kernel(specs, width, *refs):
    count = len(specs)
    sources = refs[:width]
    outs = refs[width : 2 * width]
    scratch = refs[2 * width :]
    buffers = [scratch[5 * i : 5 * i + 5] for i in range(count)]
    load_sem, send_sem, recv_sem = scratch[5 * count :]
    section = lax.axis_index("section")
    dp = lax.axis_index("dp")
    x = lax.rem(dp, 2)
    y = lax.rem(dp // 2, 2)
    z = dp // 4
    at_x = (section, dp + 1 - 2 * x)
    at_y = (section, dp + 2 - 4 * y)
    at_up = (section, dp + 4)
    at_down = (section, dp - 4)

    barrier = pltpu.get_barrier_semaphore()
    pl.semaphore_signal(barrier, inc=1, device_id=at_x, device_id_type=MESH)
    pl.semaphore_signal(barrier, inc=1, device_id=at_y, device_id_type=MESH)

    @pl.when(z < 3)
    def _():
        pl.semaphore_signal(barrier, inc=1, device_id=at_up, device_id_type=MESH)

    @pl.when(z > 0)
    def _():
        pl.semaphore_signal(barrier, inc=1, device_id=at_down, device_id_type=MESH)

    pl.semaphore_wait(barrier, 2 + jnp.where(z < 3, 1, 0) + jnp.where(z > 0, 1, 0))

    def remote(i, slot, src, dst, where):
        return pltpu.make_async_remote_copy(
            src_ref=src,
            dst_ref=dst,
            send_sem=send_sem.at[i, slot],
            recv_sem=recv_sem.at[i, slot],
            device_id=where,
            device_id_type=MESH,
        )

    def window(i):
        spec = specs[i]
        ref = sources[spec["array"]]
        (r0, rn), (c0, cn) = spec["rows"], spec["cols"]
        return ref.at[:, :, :, pl.ds(r0, rn), pl.ds(c0, cn)]

    def target(i):
        spec = specs[i]
        ref = outs[spec["array"]]
        (r0, rn), (c0, cn) = spec["rows"], spec["cols"]
        return ref.at[pl.ds(r0, rn), pl.ds(c0, cn)]

    def load(i):
        spec = specs[i]
        own = buffers[i][0]
        src = window(i)
        if spec["order"] == "xyz":
            part = src.at[:, :, x]
        elif spec["order"] == "yxz":
            part = src.at[:, y]
        else:
            part = src
        return pltpu.make_async_copy(part, own, load_sem.at[i])

    def first_copy(i):
        spec = specs[i]
        own, first, second, plus, minus = buffers[i]
        src = window(i)
        if spec["order"] == "xyz":
            return remote(i, 0, src.at[:, :, 1 - x], first, at_x)
        if spec["order"] == "yxz":
            return remote(i, 0, src.at[:, 1 - y], first, at_y)
        if spec["order"] == "zxy":
            return remote(i, 0, plus.at[z, :, 1 - x], first, at_x)
        return remote(i, 0, plus.at[z, 1 - y], first, at_y)

    def second_copy(i):
        spec = specs[i]
        own, first, second, plus, minus = buffers[i]
        if spec["order"] == "xyz":
            return remote(i, 1, first.at[:, 1 - y], second, at_y)
        if spec["order"] == "yxz":
            return remote(i, 1, first.at[:, 1 - x], second, at_x)
        if spec["order"] == "zxy":
            return remote(i, 1, first.at[1 - y], second, at_y)
        return remote(i, 1, first.at[1 - x], second, at_x)

    def add_any(dst, left, right):
        lead = dst.shape[:-2]
        total = 1
        for size in lead:
            total *= size

        def step(k, carry):
            at = []
            rest = k
            for size in reversed(lead):
                at.append(lax.rem(rest, size))
                rest = rest // size
            at = tuple(reversed(at))
            dst[at] = (left[at].astype(F32) + right[at].astype(F32)).astype(dst.dtype)
            return carry

        if total == 1:
            at = (0,) * len(lead)
            dst[at] = (left[at].astype(F32) + right[at].astype(F32)).astype(dst.dtype)
        else:
            lax.fori_loop(0, total, step, 0)

    def z_base(i):
        return buffers[i][0] if specs[i]["order"][0] == "z" else buffers[i][2]

    def up_copy(i, d, src):
        return remote(i, 2 + d, src, buffers[i][3].at[d], at_up)

    def down_copy(i, d, src):
        return remote(i, 6 + d, src, buffers[i][4].at[d], at_down)

    def z_start(i):
        base = z_base(i)

        @pl.when(z == 0)
        def _():
            for d in (3, 2, 1):
                up_copy(i, d, base.at[d]).start()

        @pl.when(z == 3)
        def _():
            for d in (0, 1, 2):
                down_copy(i, d, base.at[d]).start()

    def pass_up(i, d):
        base, plus = z_base(i), buffers[i][3]
        copy = up_copy(i, d, plus.at[d])
        copy.wait_recv()
        add_any(plus.at[d], plus.at[d], base.at[d])
        copy.start()

    def pass_down(i, d):
        base, minus = z_base(i), buffers[i][4]
        copy = down_copy(i, d, minus.at[d])
        copy.wait_recv()
        add_any(minus.at[d], minus.at[d], base.at[d])
        copy.start()

    def z_near(i):
        @pl.when(z == 1)
        def _():
            for d in (3, 2):
                pass_up(i, d)

        @pl.when(z == 2)
        def _():
            for d in (0, 1):
                pass_down(i, d)

    def z_far(i):
        @pl.when(z == 2)
        def _():
            pass_up(i, 3)

        @pl.when(z == 1)
        def _():
            pass_down(i, 0)

    def z_arrive(i):
        plus, minus = buffers[i][3], buffers[i][4]

        @pl.when(z > 0)
        def _():
            up_copy(i, z, plus.at[z]).wait_recv()

        @pl.when(z < 3)
        def _():
            down_copy(i, z, minus.at[z]).wait_recv()

    def z_sum(i, at, base):
        plus, minus = buffers[i][3], buffers[i][4]
        from_low = plus[(z,) + at].astype(F32)
        from_high = minus[(z,) + at].astype(F32)
        mine = base[(z,) + at].astype(F32)
        return mine + from_low + from_high

    def stage(i, step):
        spec = specs[i]
        own, first, second, plus, minus = buffers[i]
        order = spec["order"]
        if order[0] == "z":
            if step == 0:
                load(i).start()
            elif step == 1:
                load(i).wait()
                z_start(i)
            elif step == 2:
                z_near(i)
            elif step == 3:
                z_far(i)
            elif step == 4:
                z_arrive(i)
                for a in range(2):
                    for b in range(2):
                        plus[z, a, b] = z_sum(i, (a, b), own).astype(plus.dtype)
                first_copy(i).start()
            elif step == 5:
                first_copy(i).wait_recv()
                for a in range(2):
                    mine = plus[z, a, x] if order[1] == "x" else plus[z, y, a]
                    first[a] = (mine.astype(F32) + first[a].astype(F32)).astype(first.dtype)
                second_copy(i).start()
            elif step == 6:
                second_copy(i).wait_recv()
                mine = first[y] if order[1] == "x" else first[x]
                target(i)[...] = mine.astype(F32) + second[...].astype(F32)
        else:
            if step == 0:
                load(i).start()
                first_copy(i).start()
            elif step == 1:
                load(i).wait()
                first_copy(i).wait_recv()
                add_any(first, first, own)
                second_copy(i).start()
            elif step == 2:
                second_copy(i).wait_recv()
                mine = y if order == "xyz" else x

                def merge(k, carry):
                    second[k] = (second[k].astype(F32) + first[k, mine].astype(F32)).astype(
                        second.dtype
                    )
                    return carry

                lax.fori_loop(0, 4, merge, 0)
                z_start(i)
            elif step == 3:
                z_near(i)
            elif step == 4:
                z_far(i)
            elif step == 5:
                z_arrive(i)
                target(i)[...] = z_sum(i, (), second)

    @pl.when(z == 0)
    def _():
        for i in range(count):
            plus = buffers[i][3]
            plus[0] = jnp.zeros(plus.shape[1:], plus.dtype)

    @pl.when(z == 3)
    def _():
        for i in range(count):
            minus = buffers[i][4]
            minus[3] = jnp.zeros(minus.shape[1:], minus.dtype)

    last = max(spec["slot"] for spec in specs) + 7
    for slot in range(last):
        live = [(slot - spec["slot"], i) for i, spec in enumerate(specs)]
        live = [(step, i) for step, i in live if 0 <= step <= 6]
        for step, i in [e for e in live if e[0] == 0]:
            stage(i, step)
        for step, i in sorted([e for e in live if e[0] > 0], key=lambda e: (-e[0], e[1])):
            stage(i, step)

    for i in range(count):
        first_copy(i).wait_send()
        second_copy(i).wait_send()
        base = z_base(i)
        for d in (3, 2, 1):

            @pl.when(z < d)
            def _():
                up_copy(i, d, base.at[d]).wait_send()

        for d in (0, 1, 2):

            @pl.when(z > d)
            def _():
                down_copy(i, d, base.at[d]).wait_send()


def plan(shapes, chunks=8):
    (ur, uc), (dr, dc) = shapes[0], shapes[1]
    specs = []
    for k in range(chunks):
        wide, tall = uc // chunks, dr // chunks
        specs.append(dict(array=0, rows=(0, ur), cols=(k * wide, wide), order="xyz", slot=k))
        specs.append(dict(array=1, rows=(k * tall, tall), cols=(0, dc), order="yxz", slot=k))
    rest = [(2, 4), (3, 2), (4, 2)]
    slots = iter((0, 0, 1, 1, 2, 3, 4, 5))
    for array, parts in rest:
        height, wide = shapes[array][0], shapes[array][1] // parts
        for k in range(parts):
            order = "zxy" if k % 2 else "zyx"
            specs.append(
                dict(array=array, rows=(0, height), cols=(k * wide, wide), order=order, slot=next(slots))
            )
    height, wide = shapes[5]
    specs.append(dict(array=5, rows=(0, height), cols=(0, wide), order="xyz", slot=1))
    return specs


def reduce_scatter(arrays, collective_id=1):
    shapes = [a.shape[1:] for a in arrays]
    specs = plan(shapes)
    views = [a.reshape((4, 2, 2) + a.shape[1:]) for a in arrays]
    scratch = []
    for spec in specs:
        tile = (spec["rows"][1], spec["cols"][1])
        kind = arrays[spec["array"]].dtype
        if spec["order"][0] == "z":
            full = [(4, 2, 2), (2,), (), (4, 2, 2), (4, 2, 2)]
        else:
            full = [(4, 2), (4, 2), (4,), (4,), (4,)]
        scratch += [pltpu.VMEM(lead + tile, kind) for lead in full]
    count = len(specs)
    scratch += [
        pltpu.SemaphoreType.DMA((count,)),
        pltpu.SemaphoreType.DMA((count, 10)),
        pltpu.SemaphoreType.DMA((count, 10)),
    ]
    return pl.pallas_call(
        functools.partial(rs_kernel, specs, len(arrays)),
        out_shape=[jax.ShapeDtypeStruct(s, F32) for s in shapes],
        in_specs=[pl.BlockSpec(memory_space=pl.ANY)] * len(arrays),
        out_specs=[pl.BlockSpec(memory_space=pltpu.VMEM)] * len(arrays),
        scratch_shapes=scratch,
        compiler_params=pltpu.CompilerParams(
            collective_id=collective_id, has_side_effects=True, vmem_limit_bytes=60 * 1024 * 1024
        ),
        name="sum_shards",
    )(*views)


def media_kernel(dims, dkv, media, wkv, gain, mine, other, sums):
    patches, half = dims
    section = lax.axis_index("section")

    @pl.when(pl.program_id(0) == 0)
    def _():
        sums[...] = jnp.zeros_like(sums)

    dj = dot_rows(dkv[0], wkv[...])
    hat, factor = normed(media[0].astype(F32))
    sums[0:1, :] += jnp.sum(dj * hat, axis=0, keepdims=True)
    sums[1:2, :] += jnp.sum(dj, axis=0, keepdims=True)
    grad = norm_back(dj, hat, factor, gain[...])

    @pl.when(section == 0)
    def _():
        mine[0] = grad[:, :half]
        other[0] = grad[:, half:].astype(BF16)

    @pl.when(section == 1)
    def _():
        mine[0] = grad[:, half:]
        other[0] = grad[:, :half].astype(BF16)


def media_grads(dkv, media, wkv, gain):
    images, patches, width = media.shape
    half = width // 2
    return pl.pallas_call(
        functools.partial(media_kernel, (patches, half)),
        grid=(images,),
        out_shape=[
            jax.ShapeDtypeStruct((images, patches, half), F32),
            jax.ShapeDtypeStruct((images, patches, half), BF16),
            jax.ShapeDtypeStruct((8, width), F32),
        ],
        in_specs=[
            pl.BlockSpec((1, patches, dkv.shape[2]), lambda i: (i, 0, 0)),
            pl.BlockSpec((1, patches, width), lambda i: (i, 0, 0)),
            pl.BlockSpec(wkv.shape, lambda i: (0, 0)),
            pl.BlockSpec((1, width), lambda i: (0, 0)),
        ],
        out_specs=[
            pl.BlockSpec((1, patches, half), lambda i: (i, 0, 0)),
            pl.BlockSpec((1, patches, half), lambda i: (i, 0, 0)),
            pl.BlockSpec((8, width), lambda i: (0, 0)),
        ],
        compiler_params=pltpu.CompilerParams(vmem_limit_bytes=48 * 1024 * 1024),
        name="media_grads",
    )(dkv, media, wkv, gain)


def weight_grad(left, right):
    left = left.reshape(-1, left.shape[-1])
    right = right.reshape(-1, right.shape[-1])
    return dot_cols(left, right).astype(BF16)


def shards(
    media,
    image_live,
    start_latents,
    latent_cotangent,
    media_gain,
    media_bias,
    latent_gain,
    latent_bias,
    w_query,
    w_kv,
    w_out,
    ff_gain,
    ff_bias,
    w_up,
    w_down,
):
    images, patches, width = media.shape
    latents = start_latents.shape[0]
    peers = lax.axis_size("dp")
    rows = images * latents
    target = (latent_cotangent * image_live.astype(BF16)[:, None, None]).reshape(rows, width)
    blank = jnp.zeros((1, width), F32)
    vectors = jnp.concatenate(
        [media_gain, media_bias, latent_gain, latent_bias, ff_gain, ff_bias, blank, blank], axis=0
    )
    wq, wkv, wo, wu, wd = w_query[0], w_kv[0], w_out[0], w_up[0], w_down[0]
    y, j, o, f, h, du, dz1, dq, dkv, g, sums, start_sum = layers(
        start_latents, media, target, vectors, wq, wkv, wo, wu, wd
    )
    mine, other, media_sums = media_grads(dkv, media, wkv, media_gain)
    theirs = lax.ppermute(other, "section", [(0, 1), (1, 0)])
    grad_up = weight_grad(f, du)
    grad_down = weight_grad(h, g)
    grad_kv = weight_grad(j, dkv)
    grad_query = weight_grad(j[:, patches:], dq)
    grad_out = weight_grad(o, dz1)
    lines = jnp.concatenate([media_sums[:2], sums[2:6]], axis=0)
    if peers == 16:
        part = width // peers
        small = jnp.concatenate(
            [lines.reshape(6, peers, part).swapaxes(0, 1).reshape(peers, -1),
             start_sum.reshape(latents, peers, part).swapaxes(0, 1).reshape(peers, -1)],
            axis=1,
        )
        small = jnp.pad(small, ((0, 0), (0, 40 * 128 - small.shape[1]))).reshape(peers, 40, 128)

        def cut(a):
            return a.reshape((peers, a.shape[0] // peers) + a.shape[1:])

        up, down, kv, query, out, small = reduce_scatter(
            [cut(grad_up), cut(grad_down), cut(grad_kv), cut(grad_query), cut(grad_out), small]
        )
        small = small.reshape(-1)
        lines = small[: 6 * part].reshape(6, part)
        start_part = small[6 * part : (6 + latents) * part].reshape(latents, part)
    else:
        up, down, kv, query, out = (
            lax.psum_scatter(a, "dp", scatter_dimension=0, tiled=True).astype(F32)
            for a in (grad_up, grad_down, grad_kv, grad_query, grad_out)
        )
        lines = lax.psum_scatter(lines, "dp", scatter_dimension=1, tiled=True)
        start_part = lax.psum_scatter(start_sum, "dp", scatter_dimension=1, tiled=True)
    first = lax.axis_index("section") == 0
    half = latents // 2
    far = lax.ppermute(start_part[half:], "section", [(0, 1), (1, 0)])
    start_grad = jnp.where(first, start_part[:half], far)
    media_grad = mine + theirs.astype(F32)
    return (
        y.reshape(1, images, latents, width),
        media_grad,
        start_grad,
        lines[0:1],
        lines[1:2],
        lines[2:3],
        lines[3:4],
        query[None],
        kv[None],
        out[None],
        lines[4:5],
        lines[5:6],
        up[None],
        down[None],
    )


def solution(mesh):
    row = P("section", None)
    mat = P("section", None, None)
    in_specs = (
        P("dp", None, None), P("dp"), P(), P("dp", None, None),
        row, row, row, row, mat, mat, mat, row, row, mat, mat,
    )
    line = P("section", "dp")
    block = P("section", "dp", None)
    out_specs = (
        P("section", "dp", None, None), P("dp", None, "section"), line,
        line, line, line, line, block, block, block, line, line, block, block,
    )
    return jax.shard_map(shards, mesh=mesh, in_specs=in_specs, out_specs=out_specs, check_vma=False)
```

time: 2070 us -> 332 us (0.16)
  waiting for transfers between devices: 1270 us -> 0.01 us
  matrix products: 384 us -> 29.3 us
  Pallas kernels: 0 us -> 275 us
  other arithmetic: 190 us -> 8.81 us
  local copies, waits for them, and re-layouts: 180 us -> 13.9 us
    reduce_scatter x7 -> x0, waiting for transfers between devices: 997 us -> none  [the longest x5 970 us: shards(): lax.psum_scatter(totals, 'dp', scatter_dimension=1, tiled=True)]
    dot_general x110 -> x5, matrix products: 384 us -> 29.3 us  [dot_cols(): lax.dot_general(left, right, (((0,), (0,)), ((), ())), preferred_element_...]
    unnamed x21 -> x0, waiting for transfers between devices: 276 us -> none
    pallas_call x0 -> x3, Pallas kernels: none -> 275 us  [the longest x1 171 us: reduce_scatter(): pl.pallas_call(functools.partial(rs_kernel, specs, len(arrays)), out_shap...]
    dynamic_update_slice x62 -> x0, other arithmetic: 131 us -> none  [put_rows(): lax.dynamic_update_slice_in_dim(buffer, jnp.where(is_valid, values, forme...]
    slice x28 -> x8, local copies, waits for them, and re-layouts: 56.7 us -> 4.41 us  [the longest x1 2.26 us: shards(): grad_query = weight_grad(j[:, patches:], dq)]
    reshape x25 -> x6, local copies, waits for them, and re-layouts: 42.4 us -> 0.57 us  [the longest x2 0.32 us: shards(): start_sum.reshape(latents, peers, part).swapaxes(0, 1).reshape(peers, -1)]
    unnamed x617 -> x37, local copies, waits for them, and re-layouts: 44.1 us -> 7.35 us
  transfers between devices with their start and end apart: 22 -> 2, of which waited for: 12 -> 0; matrix products, arithmetic and copies ran while one was open for 16% -> 11% of each run, Pallas kernels for 0% -> 52%
where the time goes in v1:
time: 332 us; the launch traced here: 328 us
  Pallas kernels  275 us (83%)
  matrix products  29.3 us (9%)
  local copies, waits for them, and re-layouts  13.9 us (4%)
  other arithmetic  8.81 us (3%)
    pallas_call x1, Pallas kernels, reduce_scatter(): pl.pallas_call(functools.partial(rs_kernel, specs, len(arrays)), out_shap...  171 us
    pallas_call x1, Pallas kernels, layers(): pl.pallas_call(functools.partial(layer_kernel, dims), out_shape=out_shape...  90.3 us
    dot_general x5, matrix products, dot_cols(): lax.dot_general(left, right, (((0,), (0,)), ((), ())), preferred_element_...  29.3 us
    pallas_call x1, Pallas kernels, media_grads(): pl.pallas_call(functools.partial(media_kernel, (patches, half)), grid=(im...  13.3 us
    unnamed x37, local copies, waits for them, and re-layouts  7.35 us
  transfers between devices with their start and end apart: 2, of which 0 were waited for; matrix products, arithmetic and copies ran while one was open for 11% of the time, Pallas kernels for 52%

profile of v1, /device:TPU:10, one launch (start us, length us, event | category | flops | bytes accessed | tf_op | source)
XLA Modules:
  0.0 327.7 jit_solution(16668598587332568246)
XLA Ops:
  0.6 0.7 convert_element_type.23
  1.3 2.3 broadcast_multiply_fusion
  3.6 1.4 concatenate.13.vectors
  5.1 90.3 %layers.1 = (bf16[512,1024]{1,0:T(8,128)(2,1)}, bf16[8,320,1024]{2,1,0:T(8,128)(2,1)}, bf16[512,512]{1,0:T(8,128)(2,1)}, bf16[512,1024]{1,0:T(8,128)(2,1)}, bf16...) custom-call(bf16[64,1024]{1,0:T(8,128)(2,1)} %start.1, ...), custom_call_target="tpu_custom_call" | custom-call | tf_op jit(solution)/shard_map/layers/pallas_call | solution.py:448
  95.3 0.0 copy-done.1
  95.4 0.0 copy-start
  95.4 1.6 copy-done
  96.9 13.3 %media_grads.1 = (f32[8,256,512]{2,1,0:T(8,128)}, bf16[8,256,512]{2,1,0:T(8,128)(2,1)}, f32[8,1024]{1,0:T(8,128)S(1)}) custom-call(bf16[8,320,1024]{2,1,0:T(8,128)(2,1)} %get-tuple-element.36.dkv, bf16[8,256,1024]{2,1,0:T(8,128)(2,1)} %media.3, bf16[1024,1024]{1,0:T(8,128)(2,1)S(1)} %bitcast.39, f32[1,1024]{1,0:T(1,128)S(1)} %copy-done.1), custom_call_target="tpu_custom_call" | custom-call | tf_op jit(solution)/shard_map/media_grads/pallas_call | solution.py:823
  110.2 0.0 collective-permute-start
  110.2 2.3 slice.47
  112.5 0.0 copy-done.2
  112.5 9.5 %bitcast_convert_fusion = bf16[1024,1024]{1,0:T(8,128)(2,1)} fusion(bf16[8,320,1024]{2,1,0:T(8,128)(2,1)} %get-tuple-element.43, bf16[8,320,1024]{2,1,0:T(8,128)(2,1)S(1)} %copy-done.2), kind=kOutput, calls=%fused_computation.2 | convolution fusion | flops 5369757696 | bytes 12582912 | tf_op jit(solution)/shard_map/dot_general | solution.py:27
  122.0 0.0 copy-done.10
  122.0 0.0 copy-done.6
  122.0 0.1 reshape.68
  122.1 0.2 copy.32
  122.3 0.2 reshape.69
  122.5 0.0 copy-start.14
  122.5 0.1 reshape.66
  122.6 0.1 reshape.67
  122.7 3.2 convolution_convert_fusion.2
  126.0 3.1 convolution_convert_fusion.3
  129.0 0.0 copy-done.14
  129.0 0.0 copy-done.12
  129.0 6.8 %convolution_convert_fusion.1 = bf16[1024,4096]{1,0:T(8,128)(2,1)} fusion(bf16[512,1024]{1,0:T(8,128)(2,1)S(1)} %copy-done.14, bf16[512,4096]{1,0:T(8,128)(2,1)S(1)} %copy-done.12), kind=kOutput, calls=%fused_computation.1 | convolution fusion | flops 4299161600 | bytes 13631488 | tf_op jit(solution)/shard_map/dot_general | solution.py:27
  135.8 0.8 copy.33
  136.6 6.7 %convolution_convert_fusion = bf16[4096,1024]{1,0:T(8,128)(2,1)} fusion(bf16[512,4096]{1,0:T(8,128)(2,1)S(1)} %copy-done.11, bf16[512,1024]{1,0:T(8,128)(2,1)S(1)} %copy-done.13), kind=kOutput, calls=%fused_computation | convolution fusion | flops 4299161600 | bytes 13631488 | tf_op jit(solution)/shard_map/dot_general | solution.py:27
  143.4 171.3 %sum_shards.1 = (f32[64,4096]{1,0:T(8,128)}, f32[256,1024]{1,0:T(8,128)}, f32[64,1024]{1,0:T(8,128)}, f32[64,512]{1,0:T(8,128)}, f32[32,1024]{1,0:T(8,128)}, /*index=5*/f32[40,128]{1,0:T(8,128)}) custom-call(bf16[4,2,2,64,4096]{4,3,2,1,0:T(8,128)(2,1)} %bitcast.42, bf16[4,2,2,256,1024]{4,3,2,1,0:T(8,128)(2,1)} %bitcast.43, ...), custom_call_target="tpu_custom_call" | custom-call | tf_op jit(solution)/shard_map/sum_shards/pallas_call | solution.py:782
  314.7 0.8 fusion.1
  315.5 0.1 slice.53
  315.6 0.0 collective-permute-start.1
  315.6 0.7 slice.54
  316.2 0.1 reshape.70
  316.3 0.5 fusion.2
  316.9 0.1 slice.51
  316.9 0.0 collective-permute-done.1
  316.9 0.6 broadcast_select_fusion
  317.6 0.0 collective-permute-done
  317.6 5.2 %convert_add_fusion = f32[8,256,512]{2,1,0:T(8,128)} fusion(f32[8,256,512]{2,1,0:T(8,128)} %get-tuple-element.37, bf16[8,256,512]{2,1,0:T(8,128)(2,1)S(1)} %collective-permute-done), kind=kLoop, calls=%fused_computation.3 | loop fusion | flops 2097152 | bytes 10485760 | tf_op jit(solution)/shard_map/add | solution.py:920
  322.8 1.0 copy.42
  323.7 0.7 copy.43
  324.4 0.7 copy.44
  325.1 0.0 copy-done.8
  325.1 0.7 copy.45
  325.8 0.0 copy-done.5
  325.8 1.0 copy.46
  326.7 0.0 copy-done.4
  326.7 1.0 copy.47
  (24 shorter events, 0.1 us)
Async XLA Ops:
  5.1 90.3 %copy-start.1 = (f32[1,1024]{1,0:T(1,128)S(1)}, f32[1,1024]{1,0:T(1,128)}, u32[]{:S(2)}) copy-start(f32[1,1024]{1,0:T(1,128)} %gain.1) | copy-start | bytes 12292
  95.4 1.6 copy-start
  96.9 15.6 %copy-start.2 = (bf16[8,320,1024]{2,1,0:T(8,128)(2,1)S(1)}, bf16[8,320,1024]{2,1,0:T(8,128)(2,1)}, u32[]{:S(2)}) copy-start(bf16[8,320,1024]{2,1,0:T(8,128)(2,1)} %get-tuple-element.36.dkv) | copy-start | bytes 15728644
  110.2 207.3 %collective-permute-start = (bf16[8,256,512]{2,1,0:T(8,128)(2,1)}, bf16[8,256,512]{2,1,0:T(8,128)(2,1)S(1)}, u32[]{:S(2)}, u32[]{:S(2)}) collective-permute-start(bf16[8,256,512]{2,1,0:T(8,128)(2,1)} %get-tuple-element.38), channel_id=1, source_target_pairs={{0,16},{16,0},{1,17},{17,1},{2,18},{18,2},{3,19},{19,3},{4,20},{20... | collective-permute-start | bytes 6291464 | tf_op jit(solution)/shard_map/ppermute | solution.py:884
  112.5 9.5 %copy-start.10 = (f32[8,1024]{1,0:T(8,128)S(1)}, f32[8,1024]{1,0:T(8,128)}, u32[]{:S(2)}) copy-start(f32[8,1024]{1,0:T(8,128)} %get-tuple-element.48) | copy-start | bytes 98308
  112.5 9.5 %copy-start.6 = (f32[64,1024]{1,0:T(8,128)S(1)}, f32[64,1024]{1,0:T(8,128)}, u32[]{:S(2)}) copy-start(f32[64,1024]{1,0:T(8,128)} %get-tuple-element.49) | copy-start | bytes 786436
  122.5 6.5 %copy-start.14 = (bf16[512,1024]{1,0:T(8,128)(2,1)S(1)}, bf16[512,1024]{1,0:T(8,128)(2,1)}, u32[]{:S(2)}) copy-start(bf16[512,1024]{1,0:T(8,128)(2,1)} %get-tuple-element.39) | copy-start | bytes 3145732
  122.7 6.3 %copy-start.12 = (bf16[512,4096]{1,0:T(8,128)(2,1)S(1)}, bf16[512,4096]{1,0:T(8,128)(2,1)}, u32[]{:S(2)}) copy-start(bf16[512,4096]{1,0:T(8,128)(2,1)} %get-tuple-element.40) | copy-start | bytes 12582916
  129.0 7.6 %copy-start.11 = (bf16[512,4096]{1,0:T(8,128)(2,1)S(1)}, bf16[512,4096]{1,0:T(8,128)(2,1)}, u32[]{:S(2)}) copy-start(bf16[512,4096]{1,0:T(8,128)(2,1)} %get-tuple-element.41) | copy-start | bytes 12582916
  129.0 7.6 %copy-start.13 = (bf16[512,1024]{1,0:T(8,128)(2,1)S(1)}, bf16[512,1024]{1,0:T(8,128)(2,1)}, u32[]{:S(2)}) copy-start(bf16[512,1024]{1,0:T(8,128)(2,1)} %get-tuple-element.42) | copy-start | bytes 3145732
  315.6 1.4 collective-permute-start.1
  317.6 5.2 %copy-start.3 = (bf16[512,1024]{1,0:T(8,128)(2,1)S(1)}, bf16[512,1024]{1,0:T(8,128)(2,1)}, u32[]{:S(2)}) copy-start(bf16[512,1024]{1,0:T(8,128)(2,1)} %get-tuple-element.35) | copy-start | bytes 3145732
  317.6 6.2 %copy-start.9 = (f32[64,512]{1,0:T(8,128)S(1)}, f32[64,512]{1,0:T(8,128)}, u32[]{:S(2)}) copy-start(f32[64,512]{1,0:T(8,128)} %get-tuple-element.51) | copy-start | bytes 393220
  317.6 6.8 %copy-start.7 = (f32[64,1024]{1,0:T(8,128)S(1)}, f32[64,1024]{1,0:T(8,128)}, u32[]{:S(2)}) copy-start(f32[64,1024]{1,0:T(8,128)} %get-tuple-element.52) | copy-start | bytes 786436
  317.6 7.5 %copy-start.8 = (f32[32,1024]{1,0:T(8,128)S(1)}, f32[32,1024]{1,0:T(8,128)}, u32[]{:S(2)}) copy-start(f32[32,1024]{1,0:T(8,128)} %get-tuple-element.53) | copy-start | bytes 393220
  317.6 8.2 %copy-start.5 = (f32[64,4096]{1,0:T(8,128)S(1)}, f32[64,4096]{1,0:T(8,128)}, u32[]{:S(2)}) copy-start(f32[64,4096]{1,0:T(8,128)} %get-tuple-element.54) | copy-start | bytes 3145732
  322.8 4.0 %copy-start.4 = (f32[256,1024]{1,0:T(8,128)S(1)}, f32[256,1024]{1,0:T(8,128)}, u32[]{:S(2)}) copy-start(f32[256,1024]{1,0:T(8,128)} %get-tuple-element.55) | copy-start | bytes 3145732
